TPU v7x, 128 devices: a whole 4x4x4 slice. The times are simulated.
128 devices in a mesh: seq: 4 (over x), shard: 8 (over z_lo, y), replica: 4 (over z_hi, core).
Axes of the slice: x: 4, y: 4, z: 4 (z_hi: 2, z_lo: 2; z = z_hi * 2 + z_lo), core: 2. Of those that a mesh axis runs over, the one named last changes fastest.
Arguments:
- tokens: bfloat16 [32, 1024, 1024], P(('shard', 'replica'), 'seq'), may hold values from -6 to 6
- cotangent: bfloat16 [32, 1024, 1024], P(('shard', 'replica'), 'seq'), may hold values from -6 to 6
- w_qkv: float32 [1024, 4096], P(('seq', 'shard')), may hold values from -0.1875 to 0.1875
- w_out: float32 [2048, 1024], P(('seq', 'shard')), may hold values from -0.75 to 0.75
- w_gu: float32 [1024, 6144], P(('seq', 'shard')), may hold values from -0.1875 to 0.1875
- w_down: float32 [3072, 1024], P(('seq', 'shard')), may hold values from -0.109375 to 0.109375
- gains: float32 [2304], P(('seq', 'shard')), may hold values from 0.5 to 2, as said below
- first_qkv: float32 [1024, 4096], P(('seq', 'shard')), may hold values from -64 to 64
- first_out: float32 [2048, 1024], P(('seq', 'shard')), may hold values from -16 to 16
- first_gu: float32 [1024, 6144], P(('seq', 'shard')), may hold values from -40 to 40
- first_down: float32 [3072, 1024], P(('seq', 'shard')), may hold values from -64 to 64
- first_gains: float32 [2304], P(('seq', 'shard')), may hold values from -192 to 192
- second_qkv: float32 [1024, 4096], P(('seq', 'shard')), may hold values from 425.984 to 1736.704
- second_out: float32 [2048, 1024], P(('seq', 'shard')), may hold values from 29.4912 to 117.9648
- second_gu: float32 [1024, 6144], P(('seq', 'shard')), may hold values from 209.7152 to 851.968
- second_down: float32 [3072, 1024], P(('seq', 'shard')), may hold values from 622.592 to 2490.368
- second_gains: float32 [2304], P(('seq', 'shard')), may hold values from 3932.16 to 15400.96
Outputs:
- mixed: bfloat16 [32, 1024, 1024], P(('shard', 'replica'), 'seq')
- input_grad: float32 [32, 1024, 1024], P(('shard', 'replica'), 'seq')
- new_qkv: float32 [1024, 4096], P(('seq', 'shard'))
- new_first_qkv: float32 [1024, 4096], P(('seq', 'shard'))
- new_second_qkv: float32 [1024, 4096], P(('seq', 'shard'))
- new_out: float32 [2048, 1024], P(('seq', 'shard'))
- new_first_out: float32 [2048, 1024], P(('seq', 'shard'))
- new_second_out: float32 [2048, 1024], P(('seq', 'shard'))
- new_gu: float32 [1024, 6144], P(('seq', 'shard'))
- new_first_gu: float32 [1024, 6144], P(('seq', 'shard'))
- new_second_gu: float32 [1024, 6144], P(('seq', 'shard'))
- new_down: float32 [3072, 1024], P(('seq', 'shard'))
- new_first_down: float32 [3072, 1024], P(('seq', 'shard'))
- new_second_down: float32 [3072, 1024], P(('seq', 'shard'))
- new_gains: float32 [2304], P(('seq', 'shard'))
- new_first_gains: float32 [2304], P(('seq', 'shard'))
- new_second_gains: float32 [2304], P(('seq', 'shard'))
Inputs may be any that keep to these rules, and one draw needn't show every extreme that they name: Positive gains.
All inputs are finite; a program needn't handle non-finite values.
Results may differ from a plain program's by a relative error of at most 0.015.
The roundings to bfloat16 on the way count: a program that leaves them out, or rounds other values in their place, can miss the bound.
Values may be sent and summed in bfloat16 or wider, within the bound.
No kernel may reach another device: no remote copies, remote signals or barrier semaphores. Data moves between devices by JAX's collectives and lax.ppermute only.
A program may use at most 384 MiB of HBM per device.

v0:
```python
import math

import jax
import jax.numpy as jnp
from jax import lax
from jax.sharding import PartitionSpec as P

HEADS = 16
KVH = 8
HD = 128
FF = 3072
STEP = 10


EPS = 1e-06
THETA = 1000000.0
BETA_ONE = 0.9
BETA_TWO = 0.95
ADAM_EPS = 1e-08
RATES = (0.04, 0.2, 0.04, 0.03, 0.4)
DECAYS = (0.1, 0.1, 0.1, 0.1, 0.0)
NEG_FILL = -1e30


def laid_out(blocks, dim):
    blocks = jnp.moveaxis(blocks, 0, dim)
    shape = blocks.shape
    return blocks.reshape(*shape[:dim], shape[dim] * shape[dim + 1], *shape[dim + 2 :])


def one_gather(arrays, axis, dims):
    flat = jnp.concatenate([a.reshape(-1) for a in arrays])
    lines, at, done = (lax.all_gather(flat, axis), 0, [])
    for a, dim in zip(arrays, dims):
        blocks = lines[:, at : at + a.size].reshape(-1, *a.shape)
        done.append(laid_out(blocks, dim))
        at += a.size
    return tuple(done)


def split_up(array, dim, size):
    shape = array.shape
    blocks = array.reshape(*shape[:dim], size, shape[dim] // size, *shape[dim + 1 :])
    return jnp.moveaxis(blocks, dim, 0)


def sum_packed(arrays, axis, dims):
    size = lax.axis_size(axis)
    blocks = [split_up(a, dim, size) for a, dim in zip(arrays, dims)]
    lines = jnp.concatenate([b.reshape(size, -1) for b in blocks], axis=1)
    span = max(16, -(-lines.shape[1] // 1024) * 8)
    lines = jnp.pad(lines, ((0, 0), (0, span * 128 - lines.shape[1]))).reshape(-1, 128)
    flat, at, done = (lax.psum_scatter(lines, axis, tiled=True).reshape(-1), 0, [])
    for b in blocks:
        part = b[0]
        done.append(flat[at : at + part.size].reshape(part.shape))
        at += part.size
    return tuple(done)


def rms_scale(value, gain):
    return value * lax.rsqrt(jnp.mean(value * value, axis=-1, keepdims=True) + EPS) * gain


def rotary(positions, half_dim):
    frequency = THETA ** (-jnp.arange(half_dim, dtype=jnp.float32) / half_dim)
    angles = positions[:, None] * frequency[None, :]
    return (jnp.cos(angles)[:, None, :], jnp.sin(angles)[:, None, :])


def rotate(value, cos_table, sin_table):
    half_dim = value.shape[-1] // 2
    lower = value[..., :half_dim]
    upper = value[..., half_dim:]
    return jnp.concatenate(
        [lower * cos_table - upper * sin_table, upper * cos_table + lower * sin_table], axis=-1
    )


def swiglu(gate_part, up_part):
    return jax.nn.silu(gate_part) * up_part


def linear(left, right):
    return jnp.dot(left, right, preferred_element_type=jnp.float32)


def contract_rows(left, right):
    return lax.dot_general(
        left, right, (((0,), (0,)), ((), ())), preferred_element_type=jnp.float32
    )


def times_transposed(left, right):
    return lax.dot_general(
        left, right, (((1,), (1,)), ((), ())), preferred_element_type=jnp.float32
    )


def attend(queries, keys_all, values_all, query_pos, key_pos):
    scores = jnp.einsum("qkgd,skd->kgqs", queries, keys_all, preferred_element_type=jnp.float32)
    causal = key_pos[None, :] <= query_pos[:, None]
    scores = jnp.where(causal, scores, NEG_FILL)
    row_top = jnp.max(scores, axis=-1, keepdims=True)
    exponent = jnp.exp(scores - row_top)
    row_total = jnp.sum(exponent, axis=-1, keepdims=True)
    weights_low = (exponent / row_total).astype(jnp.bfloat16)
    attended = jnp.einsum(
        "kgqs,skd->qkgd", weights_low, values_all, preferred_element_type=jnp.float32
    )
    return (attended, row_top + jnp.log(row_total))


def attend_back(queries, keys_all, values_all, grad_attended, log_total, query_pos, key_pos):
    scores = jnp.einsum("qkgd,skd->kgqs", queries, keys_all, preferred_element_type=jnp.float32)
    causal = key_pos[None, :] <= query_pos[:, None]
    scores = jnp.where(causal, scores, NEG_FILL)
    probs_full = jnp.exp(scores - log_total)
    grad_probs = jnp.einsum(
        "qkgd,skd->kgqs", grad_attended, values_all, preferred_element_type=jnp.float32
    )
    inner_sum = jnp.sum(probs_full * grad_probs, axis=-1, keepdims=True)
    grad_scores = (probs_full * (grad_probs - inner_sum)).astype(jnp.bfloat16)
    grad_query = jnp.einsum(
        "kgqs,skd->qkgd", grad_scores, keys_all, preferred_element_type=jnp.float32
    )
    grad_key = jnp.einsum(
        "kgqs,qkgd->skd", grad_scores, queries, preferred_element_type=jnp.float32
    )
    grad_value = jnp.einsum(
        "kgqs,qkgd->skd",
        probs_full.astype(jnp.bfloat16),
        grad_attended,
        preferred_element_type=jnp.float32,
    )
    return (grad_query, grad_key, grad_value)


def adamw(weight, gradient, first_moment, second_moment, rate, decay_rate):
    first_moment = BETA_ONE * first_moment + (1.0 - BETA_ONE) * gradient
    second_moment = BETA_TWO * second_moment + (1.0 - BETA_TWO) * gradient * gradient
    first_hat = first_moment / (1.0 - BETA_ONE**STEP)
    second_hat = second_moment / (1.0 - BETA_TWO**STEP)
    weight = weight - rate * (first_hat / (jnp.sqrt(second_hat) + ADAM_EPS) + decay_rate * weight)
    return (weight, first_moment, second_moment)


def on_device(
    tokens,
    cotangent,
    w_qkv,
    w_out,
    w_gu,
    w_down,
    gains,
    first_qkv,
    first_out,
    first_gu,
    first_down,
    first_gains,
    second_qkv,
    second_out,
    second_gu,
    second_down,
    second_gains,
):
    seqs_here, span_len, model_width = tokens.shape
    row_count = seqs_here * span_len
    group_size = HEADS // KVH
    q_width = HEADS * HD
    kv_width = KVH * HD
    length = span_len * lax.axis_size("seq")
    seq_index = lax.axis_index("seq")
    query_pos = seq_index * span_len + jnp.arange(span_len, dtype=jnp.int32)
    key_pos = jnp.arange(length, dtype=jnp.int32)
    cos_table, sin_table = rotary(query_pos.astype(jnp.float32), HD // 2)
    factor = 1.0 / math.sqrt(HD)

    def query_key(queries, keys_pre, gain_query, gain_key):
        rot_q = rotate(rms_scale(queries, gain_query), cos_table, sin_table) * factor
        rot_k = rotate(rms_scale(keys_pre, gain_key), cos_table, sin_table)
        return (rot_q, rot_k)

    big_qkv, big_out, all_gains = (
        lax.all_gather(w_qkv.astype(jnp.bfloat16), ("seq", "shard"), axis=0, tiled=True),
        lax.all_gather(w_out.astype(jnp.bfloat16), ("seq", "shard"), axis=0, tiled=True),
        lax.all_gather(gains.astype(jnp.bfloat16), ("seq", "shard"), axis=0, tiled=True),
    )
    gain_vals = all_gains.astype(jnp.float32)
    gain_one = gain_vals[:model_width]
    gain_two = gain_vals[model_width : 2 * model_width]
    gain_query = gain_vals[2 * model_width : 2 * model_width + HD]
    gain_key = gain_vals[2 * model_width + HD :]
    inputs = tokens.astype(jnp.float32).reshape(row_count, model_width)
    low_one = rms_scale(inputs, gain_one).astype(jnp.bfloat16)
    projected = linear(low_one, big_qkv)
    queries_pre = projected[:, :q_width].reshape(seqs_here, span_len, HEADS, HD)
    keys_pre = projected[:, q_width : q_width + kv_width].reshape(seqs_here, span_len, KVH, HD)
    values_pre = projected[:, q_width + kv_width :]
    rot_q, rot_k = query_key(queries_pre, keys_pre, gain_query, gain_key)
    low_q = rot_q.astype(jnp.bfloat16).reshape(seqs_here, span_len, KVH, group_size, HD)
    low_k = rot_k.astype(jnp.bfloat16).reshape(seqs_here, span_len, kv_width)
    low_v = values_pre.astype(jnp.bfloat16).reshape(seqs_here, span_len, kv_width)
    all_keys, all_values = (
        lax.all_gather(low_k, "seq", axis=1, tiled=True),
        lax.all_gather(low_v, "seq", axis=1, tiled=True),
    )
    all_keys = all_keys.reshape(seqs_here, length, KVH, HD)
    all_values = all_values.reshape(seqs_here, length, KVH, HD)

    def forward_one(pieces):
        return attend(pieces[0], pieces[1], pieces[2], query_pos, key_pos)

    attended, log_total = lax.map(forward_one, (low_q, all_keys, all_values))
    low_att = attended.reshape(row_count, q_width).astype(jnp.bfloat16)
    state = inputs + linear(low_att, big_out)
    big_gu, big_down = one_gather(
        (w_gu.astype(jnp.bfloat16), w_down.astype(jnp.bfloat16)), ("seq", "shard"), (0, 0)
    )
    low_two = rms_scale(state, gain_two).astype(jnp.bfloat16)
    gate_up = linear(low_two, big_gu)
    gate_part = gate_up[:, :FF]
    up_part = gate_up[:, FF:]
    low_hidden = swiglu(gate_part, up_part).astype(jnp.bfloat16)
    mixed = state + linear(low_hidden, big_down)
    mixed_out = mixed.astype(jnp.bfloat16).reshape(seqs_here, span_len, model_width)
    grad_mix = cotangent.reshape(row_count, model_width)
    back_gu, back_down = (big_gu, big_down)
    grad_down = contract_rows(low_hidden, grad_mix)
    grad_hidden = times_transposed(grad_mix, back_down)
    unused_out, swiglu_pull = jax.vjp(swiglu, gate_part, up_part)
    grad_gate, grad_up = swiglu_pull(grad_hidden)
    low_grad_gu = jnp.concatenate([grad_gate, grad_up], axis=1).astype(jnp.bfloat16)
    grad_gu = contract_rows(low_two, low_grad_gu)
    grad_normed_two = times_transposed(low_grad_gu, back_gu)
    unused_two, norm_pull_two = jax.vjp(rms_scale, state, gain_two)
    grad_state_norm, grad_gain_two = norm_pull_two(grad_normed_two)
    grad_state = grad_mix.astype(jnp.float32) + grad_state_norm
    own_gu, own_down = sum_packed((grad_gu, grad_down), ("seq", "shard", "replica"), (0, 0))
    back_qkv, back_out = (big_qkv, big_out)
    low_grad_state = grad_state.astype(jnp.bfloat16)
    grad_out = contract_rows(low_att, low_grad_state)
    low_grad_att = (
        times_transposed(low_grad_state, back_out)
        .astype(jnp.bfloat16)
        .reshape(seqs_here, span_len, KVH, group_size, HD)
    )

    def backward_one(pieces):
        return attend_back(
            pieces[0], pieces[1], pieces[2], pieces[3], pieces[4], query_pos, key_pos
        )

    grad_query, grad_key_all, grad_value_all = lax.map(
        backward_one, (low_q, all_keys, all_values, low_grad_att, log_total)
    )
    grad_key, grad_value = (
        lax.psum_scatter(
            grad_key_all.reshape(seqs_here, length, kv_width),
            "seq",
            scatter_dimension=1,
            tiled=True,
        ),
        lax.psum_scatter(
            grad_value_all.reshape(seqs_here, length, kv_width),
            "seq",
            scatter_dimension=1,
            tiled=True,
        ),
    )
    unused_three, query_key_pull = jax.vjp(query_key, queries_pre, keys_pre, gain_query, gain_key)
    grad_q_pre, grad_k_pre, grad_gain_query, grad_gain_key = query_key_pull(
        (
            grad_query.reshape(seqs_here, span_len, HEADS, HD),
            grad_key.reshape(seqs_here, span_len, KVH, HD),
        )
    )
    low_grad_qkv = jnp.concatenate(
        [
            grad_q_pre.reshape(row_count, q_width),
            grad_k_pre.reshape(row_count, kv_width),
            grad_value.reshape(row_count, kv_width),
        ],
        axis=1,
    ).astype(jnp.bfloat16)
    grad_qkv = contract_rows(low_one, low_grad_qkv)
    grad_normed_one = times_transposed(low_grad_qkv, back_qkv)
    unused_four, norm_pull_one = jax.vjp(rms_scale, inputs, gain_one)
    grad_input_norm, grad_gain_one = norm_pull_one(grad_normed_one)
    input_grad = (grad_state + grad_input_norm).reshape(seqs_here, span_len, model_width)
    grad_gains = jnp.concatenate([grad_gain_one, grad_gain_two, grad_gain_query, grad_gain_key])
    own_qkv, own_out, own_gains = sum_packed(
        (grad_qkv, grad_out, grad_gains), ("seq", "shard", "replica"), (0, 0, 0)
    )
    total_qkv, total_out, total_gu, total_down, total_gains = (
        lax.all_gather(own_qkv, "replica", axis=0, tiled=True),
        lax.all_gather(own_out, "replica", axis=0, tiled=True),
        lax.all_gather(own_gu, "replica", axis=0, tiled=True),
        lax.all_gather(own_down, "replica", axis=0, tiled=True),
        lax.all_gather(own_gains, "replica", axis=0, tiled=True),
    )
    upd_qkv = adamw(w_qkv, total_qkv, first_qkv, second_qkv, RATES[0], DECAYS[0])
    upd_out = adamw(w_out, total_out, first_out, second_out, RATES[1], DECAYS[1])
    upd_gu = adamw(w_gu, total_gu, first_gu, second_gu, RATES[2], DECAYS[2])
    upd_down = adamw(w_down, total_down, first_down, second_down, RATES[3], DECAYS[3])
    upd_gains = adamw(gains, total_gains, first_gains, second_gains, RATES[4], DECAYS[4])
    return (
        mixed_out,
        input_grad,
        upd_qkv[0],
        upd_qkv[1],
        upd_qkv[2],
        upd_out[0],
        upd_out[1],
        upd_out[2],
        upd_gu[0],
        upd_gu[1],
        upd_gu[2],
        upd_down[0],
        upd_down[1],
        upd_down[2],
        upd_gains[0],
        upd_gains[1],
        upd_gains[2],
    )


def solution(mesh):
    placed = (
        P(("shard", "replica"), "seq", None),
        P(("shard", "replica"), "seq", None),
        P(("seq", "shard"), None),
        P(("seq", "shard"), None),
        P(("seq", "shard"), None),
        P(("seq", "shard"), None),
        P(("seq", "shard")),
        P(("seq", "shard"), None),
        P(("seq", "shard"), None),
        P(("seq", "shard"), None),
        P(("seq", "shard"), None),
        P(("seq", "shard")),
        P(("seq", "shard"), None),
        P(("seq", "shard"), None),
        P(("seq", "shard"), None),
        P(("seq", "shard"), None),
        P(("seq", "shard")),
    )
    return jax.shard_map(
        on_device,
        mesh=mesh,
        in_specs=placed,
        out_specs=(
            P(("shard", "replica"), "seq", None),
            P(("shard", "replica"), "seq", None),
            P(("seq", "shard"), None),
            P(("seq", "shard"), None),
            P(("seq", "shard"), None),
            P(("seq", "shard"), None),
            P(("seq", "shard"), None),
            P(("seq", "shard"), None),
            P(("seq", "shard"), None),
            P(("seq", "shard"), None),
            P(("seq", "shard"), None),
            P(("seq", "shard"), None),
            P(("seq", "shard"), None),
            P(("seq", "shard"), None),
            P(("seq", "shard")),
            P(("seq", "shard")),
            P(("seq", "shard")),
        ),
        check_vma=False,
    )
```

profile of v0, /device:TPU:1, one launch (start us, length us, event | category | flops | bytes accessed | tf_op | source)
XLA Modules:
  0.0 1902.9 jit_solution(4291122402765415789)
XLA Ops:
  11.9 74.7 %all-reduce.5 = bf16[2304]{0:T(1024)(128)(2,1)S(1)} all-reduce(bf16[2304]{0:T(1024)(128)(2,1)S(1)} %dynamic-update-slice), channel_id=1, replica_groups=mesh['seq'=4,'shard'=8,'replica'=4] {'seq','shard'}, use_global_device_ids=true, to_apply=%add.5 | all-reduce | flops 2304 | bytes 9216
  88.4 73.9 %all-gather.8.cloned.1.call-done = bf16[1024,4096]{1,0:T(8,128)(2,1)} async-done(((bf16[32,4096]{1,0:T(8,128)(2,1)}), bf16[1024,4096]{1,0:T(8,128)(2,1)}) %all-gather.8.cloned.1.call-update) | async-done | bytes 8388624 | tf_op jit(solution)/shard_map/all_gather | solution.py:185
  186.0 35.7 %all-gather.14.cloned.1.call-done = bf16[1024,1024]{1,0:T(8,128)(2,1)} async-done(((bf16[256,1024]{1,0:T(8,128)(2,1)}), bf16[1024,1024]{1,0:T(8,128)(2,1)}) %all-gather.14.cloned.1.call-update) | async-done | bytes 2097168 | tf_op jit(solution)/shard_map/all_gather | solution.py:206
  225.3 32.3 %all-gather.10.cloned.1.call-done = bf16[1,1024,1024]{1,2,0:T(8,128)(2,1)} async-done(((bf16[1,256,1024]{1,2,0:T(8,128)(2,1)}), bf16[1,1024,1024]{1,2,0:T(8,128)(2,1)}) %all-gather.10.cloned.1.call-update) | async-done | bytes 2097168 | tf_op jit(solution)/shard_map/all_gather | solution.py:205
  286.2 113.2 %all-gather.12.cloned.1.call-done = bf16[2048,1024]{1,0:T(8,128)(2,1)} async-done(((bf16[64,1024]{1,0:T(8,128)(2,1)}), bf16[2048,1024]{1,0:T(8,128)(2,1)}) %all-gather.12.cloned.1.call-update) | async-done | bytes 4194320 | tf_op jit(solution)/shard_map/all_gather | solution.py:186
  403.3 230.0 %all-gather.16.cloned.1.call-done = bf16[9437184]{0:T(1024)(128)(2,1)} async-done(((bf16[294912]{0:T(1024)(128)(2,1)}), bf16[9437184]{0:T(1024)(128)(2,1)}) %all-gather.16.cloned.1.call-update) | async-done | bytes 18874384 | tf_op jit(solution)/shard_map/all_gather | solution.py:33
  633.3 25.9 %reshape.494 = bf16[32,294912]{1,0:T(8,128)(2,1)} reshape(bf16[9437184]{0:T(1024)(128)(2,1)} %all-gather.16.cloned.1.call-done) | data formatting | bytes 37748736 | tf_op jit(solution)/shard_map/all_gather | solution.py:33
  675.4 12.1 reshape_reshape.18
  721.7 11.7 fusion.6
  733.5 11.9 fusion
  745.4 12.4 fusion.2
  807.8 19.1 %reduce-scatter.4.cloned.1.call-done = f32[1,256,1024]{1,2,0:T(8,128)} async-done(((f32[1,1024,1024]{1,2,0:T(8,128)}), f32[1,256,1024]{1,2,0:T(8,128)}) %reduce-scatter.4.cloned.1.call-update) | async-done | bytes 1048592 | tf_op jit(solution)/shard_map/reduce_scatter | solution.py:258
  850.1 18.2 reshape_reshape.20
  868.3 18.6 select_maximum_fusion
  886.9 23.4 %reshape.484 = f32[50176,128]{1,0:T(8,128)} reshape(f32[128,50176]{1,0:T(8,128)} %select_maximum_fusion) | data formatting | bytes 51380224 | tf_op jit(solution)/shard_map/reshape | solution.py:52
  918.3 12.8 reshape_reshape.23
  931.1 12.8 fusion.20
  943.9 24.1 %reshape_reshape.22 = f32[128,49152]{1,0:T(8,128)} reshape(f32[1024,6144]{1,0:T(8,128)} %fusion.20) | data formatting | bytes 50331648 | tf_op jit(solution)/shard_map/reshape;reshape | solution.py:50
  968.1 25.4 %pad_maximum_fusion = f32[128,73728]{1,0:T(8,128)} fusion(f32[128,24576]{1,0:T(8,128)} %reshape_reshape.23, f32[128,49152]{1,0:T(8,128)} %reshape_reshape.22), kind=kLoop, calls=%fused_computation | loop fusion | flops 9437184 | bytes 75497472 | tf_op jit(solution)/shard_map/concatenate | solution.py:50
  993.5 31.0 %reshape.487 = f32[73728,128]{1,0:T(8,128)} reshape(f32[128,73728]{1,0:T(8,128)} %pad_maximum_fusion) | data formatting | bytes 75497472 | tf_op jit(solution)/shard_map/reshape | solution.py:52
  1033.4 109.4 %all-reduce.10.cloned.1.call-done = f32[50176,128]{1,0:T(8,128)} async-done(((f32[50176,128]{1,0:T(8,128)}), f32[50176,128]{1,0:T(8,128)}) %all-reduce.10.cloned.1.call-update) | async-done | bytes 25690128
  1164.0 11.6 all_gather.43
  1179.9 686.2 %reduce-scatter.8.cloned.1.call-done = f32[576,128]{1,0:T(8,128)} async-done(((f32[73728,128]{1,0:T(8,128)}), f32[576,128]{1,0:T(8,128)}) %reduce-scatter.8.cloned.1.call-update) | async-done | bytes 294928 | tf_op jit(solution)/shard_map/reduce_scatter | solution.py:53
  1868.0 13.5 all_gather.46
  (264 shorter events, 246.0 us)
Async XLA Ops:
  7.2 155.2 %all-gather.8.cloned.1.call-start = ((), (), s32[]{:S(2)}) async-start(), calls=%async_computation.3 | async-start | bytes 8650752 | tf_op jit(solution)/shard_map/all_gather | solution.py:185
  9.0 212.7 %all-gather.14.cloned.1.call-start = ((), (), s32[]{:S(2)}) async-start(), calls=%async_computation.9 | async-start | bytes 2621440 | tf_op jit(solution)/shard_map/all_gather | solution.py:206
  88.4 79.9 %copy-start.50 = (f32[256]{0:T(256)}, f32[256]{0:T(256)S(1)}, u32[]{:S(2)}) copy-start(f32[256]{0:T(256)S(1)} %fusion.61) | copy-start | bytes 3076
  88.4 79.9 %copy-start.43 = (f32[1024]{0:T(1024)}, f32[1024]{0:T(1024)S(1)}, u32[]{:S(2)}) copy-start(f32[1024]{0:T(1024)S(1)} %get-tuple-element.113) | copy-start | bytes 12292
  171.3 86.3 %all-gather.10.cloned.1.call-start = ((), (), s32[]{:S(2)}) async-start(), calls=%async_computation.4 | async-start | bytes 2621440 | tf_op jit(solution)/shard_map/all_gather | solution.py:205
  172.0 11.3 copy-start.17
  177.2 222.2 %all-gather.12.cloned.1.call-start = ((), (), s32[]{:S(2)}) async-start(), calls=%async_computation.5 | async-start | bytes 4325376 | tf_op jit(solution)/shard_map/all_gather | solution.py:186
  177.9 455.4 %all-gather.16.cloned.1.call-start = ((), (), s32[]{:S(2)}) async-start(), calls=%async_computation.10 | async-start | bytes 19464192 | tf_op jit(solution)/shard_map/all_gather | solution.py:33
  179.1 626.5 %reduce-scatter.6.cloned.1.call-start = ((), (), s32[]{:S(2)}) async-start(), calls=%async_computation.7 | async-start | bytes 5242880 | tf_op jit(solution)/shard_map/reduce_scatter | solution.py:264
  276.2 123.2 %copy-start.13 = (bf16[1,256,1024]{2,1,0:T(8,128)(2,1)S(1)}, bf16[1,256,1024]{2,1,0:T(8,128)(2,1)}, u32[]{:S(2)}) copy-start(bf16[1,256,1024]{2,1,0:T(8,128)(2,1)} %param.17) | copy-start | bytes 1572868
  733.4 93.5 %reduce-scatter.4.cloned.1.call-start = ((), (), s32[]{:S(2)}) async-start(), calls=%async_computation.6 | async-start | bytes 5242880 | tf_op jit(solution)/shard_map/reduce_scatter | solution.py:258
  762.9 379.9 %all-reduce.10.cloned.1.call-start = ((), (), s32[]{:S(2)}) async-start(), calls=%async_computation.11 | async-start | bytes 51380224
  910.4 955.8 %reduce-scatter.8.cloned.1.call-start = ((), (), s32[]{:S(2)}) async-start(), calls=%async_computation.8 | async-start | bytes 38043648 | tf_op jit(solution)/shard_map/reduce_scatter | solution.py:53
  1032.0 143.5 %copy-start.59 = (f32[72]{0:T(128)S(1)}, f32[72]{0:T(128)}, u32[]{:S(2)}) copy-start(f32[72]{0:T(128)} %param.23) | copy-start | bytes 868
  1032.0 143.5 %copy-start.60 = (f32[72]{0:T(128)S(1)}, f32[72]{0:T(128)}, u32[]{:S(2)}) copy-start(f32[72]{0:T(128)} %param.28) | copy-start | bytes 868
  1032.0 143.5 %copy-start.61 = (f32[72]{0:T(128)S(1)}, f32[72]{0:T(128)}, u32[]{:S(2)}) copy-start(f32[72]{0:T(128)} %param.33) | copy-start | bytes 868
  1032.0 144.1 %copy-start.39 = (f32[64,1024]{1,0:T(8,128)S(1)}, f32[64,1024]{1,0:T(8,128)}, u32[]{:S(2)}) copy-start(f32[64,1024]{1,0:T(8,128)} %param.20) | copy-start | bytes 786436
  1032.0 144.1 %copy-start.45 = (f32[64,1024]{1,0:T(8,128)S(1)}, f32[64,1024]{1,0:T(8,128)}, u32[]{:S(2)}) copy-start(f32[64,1024]{1,0:T(8,128)} %param.25) | copy-start | bytes 786436
  1032.0 144.1 %copy-start.46 = (f32[64,1024]{1,0:T(8,128)S(1)}, f32[64,1024]{1,0:T(8,128)}, u32[]{:S(2)}) copy-start(f32[64,1024]{1,0:T(8,128)} %param.30) | copy-start | bytes 786436
  1032.0 145.1 %copy-start.28 = (f32[32,4096]{1,0:T(8,128)S(1)}, f32[32,4096]{1,0:T(8,128)}, u32[]{:S(2)}) copy-start(f32[32,4096]{1,0:T(8,128)} %param.19) | copy-start | bytes 1572868
  1175.5 716.2 %copy-start.37 = (f32[96,1024]{1,0:T(8,128)S(1)}, f32[96,1024]{1,0:T(8,128)}, u32[]{:S(2)}) copy-start(f32[96,1024]{1,0:T(8,128)} %param.22) | copy-start | bytes 1179652
  1177.1 717.0 %copy-start.23 = (f32[32,6144]{1,0:T(8,128)S(1)}, f32[32,6144]{1,0:T(8,128)}, u32[]{:S(2)}) copy-start(f32[32,6144]{1,0:T(8,128)} %param.21) | copy-start | bytes 2359300
  1177.1 717.0 %copy-start.41 = (f32[32,6144]{1,0:T(8,128)S(1)}, f32[32,6144]{1,0:T(8,128)}, u32[]{:S(2)}) copy-start(f32[32,6144]{1,0:T(8,128)} %param.26) | copy-start | bytes 2359300
  1177.1 717.0 %copy-start.42 = (f32[32,6144]{1,0:T(8,128)S(1)}, f32[32,6144]{1,0:T(8,128)}, u32[]{:S(2)}) copy-start(f32[32,6144]{1,0:T(8,128)} %param.31) | copy-start | bytes 2359300
  (50 other events, 210.3 us)
Sparse Core Ops, SparseCore 0:
  10.2 152.0 all-gather.7
  171.4 50.2 all-gather.13
  223.9 33.6 all-gather.9
  259.7 139.6 all-gather.11
  401.4 231.8 all-gather.15
  733.6 44.2 reduce-scatter.5
  780.4 46.5 reduce-scatter.3
  910.5 232.2 all-reduce.9
  1145.4 720.6 reduce-scatter.7
where the time goes:
time: 1910 us; the launch traced here: 1900 us
  waiting for transfers between devices  1300 us (68%)
  local copies, waits for them, and re-layouts  225 us (12%)
  blocking collectives  128 us (7%)
  matrix products  128 us (7%)
  other arithmetic  104 us (5%)
    reduce_scatter x1, waiting for transfers between devices, sum_packed(): lax.psum_scatter(lines, axis, tiled=True).reshape(-1)  686 us
    all_gather x1, waiting for transfers between devices, one_gather(): lines, at, done = (lax.all_gather(flat, axis), 0, [])  230 us
    all_gather x1, waiting for transfers between devices, on_device(): lax.all_gather(w_out.astype(jnp.bfloat16), ('seq', 'shard'), axis=0, tile...  113 us
    unnamed x10, waiting for transfers between devices  110 us
    unnamed x2, blocking collectives  81.7 us
    all_gather x1, waiting for transfers between devices, on_device(): lax.all_gather(w_qkv.astype(jnp.bfloat16), ('seq', 'shard'), axis=0, tile...  73.9 us
    another operation x4, local copies, waits for them, and re-layouts, sum_packed(): lines = jnp.concatenate([b.reshape(size, -1) for b in blocks], axis=1)  64.9 us
    reshape x2, local copies, waits for them, and re-layouts, sum_packed(): jnp.pad(lines, ((0, 0), (0, span * 128 - lines.shape[1]))).reshape(-1, 128)  54.4 us
  transfers between devices with their start and end apart: 9, of which 8 were waited for; matrix products, arithmetic and copies ran while one was open for 13% of the time, Pallas kernels for 0%

commit v1 on v0

v1 whole, which is shorter than its diff:
```python
import math

import jax
import jax.numpy as jnp
import numpy as np
from jax import lax
from jax.experimental import pallas as pl
from jax.experimental.pallas import tpu as pltpu
from jax.sharding import PartitionSpec as P

HEADS = 16
KVH = 8
HD = 128
FF = 3072
STEP = 10
EPS = 1e-06
THETA = 1000000.0
BETA_ONE = 0.9
BETA_TWO = 0.95
ADAM_EPS = 1e-08
RATES = (0.04, 0.2, 0.04, 0.03, 0.4)
DECAYS = (0.1, 0.1, 0.1, 0.1, 0.0)
NEG_FILL = -1e30

AXES = ("seq", "shard", "replica")
DEVICES = 128
BLOCK = 256
BF = jnp.bfloat16
F32 = jnp.float32
VMEM_LIMIT = 56 * 1024 * 1024


def place_of(device):
    replica, shard, x = device % 4, (device // 4) % 8, device // 32
    return x, shard % 4, (replica // 2) * 2 + shard // 4, replica % 2


def device_at(x, y, z, k):
    return (x * 8 + (z % 2) * 4 + y) * 4 + (z // 2) * 2 + k


def flip(dim, x, y, z, k):
    return {
        "a": (x ^ 1, y, z, k),
        "b": (3 - x, y, z, k),
        "c": (x, y ^ 1, z, k),
        "d": (x, 3 - y, z, k),
        "e": (x, y, z ^ 1, k),
        "f": (x, y, 3 - z, k),
        "h": (x, y, z ^ 2, k),
        "k": (x, y, z, k ^ 1),
    }[dim]


def quarter_of(x, k):
    return k if x < 2 else 3 - k


def partners(dims):
    pairs = []
    for device in range(DEVICES):
        place = place_of(device)
        pairs.append((device, device_at(*flip(dims[place[3]], *place))))
    return pairs


def swap(value, dims):
    return lax.ppermute(value, AXES, partners(dims))


def home_pairs():
    pairs = []
    for device in range(DEVICES):
        x, y, z, k = place_of(device)
        moved = {(0, 1): (1, 0), (1, 0): (0, 1), (2, 0): (3, 1), (3, 1): (2, 0)}.get((x, k), (x, k))
        pairs.append((device, device_at(moved[0], y, z, moved[1])))
    return pairs


def rehome(value):
    return lax.ppermute(value, AXES, home_pairs())


def spread(value, steps):
    for dims in steps:
        value = jnp.concatenate([value, swap(value, dims)], axis=0)
    return value


def shard_of(place):
    return (place[2] % 2) * 4 + place[1]


def slot_places(device, steps):
    places = [place_of(device)]
    for dims in steps:
        places = places + [flip(dims[p[3]], *p) for p in places]
    return places


def row_table(steps):
    table = np.zeros((DEVICES, 32), np.int32)
    for device in range(DEVICES):
        slots = slot_places(device, ("bb", "aa") + tuple(steps))
        table[device] = [p[0] * 8 + shard_of(p) for p in slots]
    return table


def shard_table(steps):
    table = np.zeros((DEVICES, 8), np.int32)
    for device in range(DEVICES):
        table[device] = [shard_of(p) for p in slot_places(device, steps)]
    return table


STEPS_Q = ("cd", "ef", "dc")
STEPS_KV = ("dc", "cd", "ef")
STEPS_ROWS = ("cd", "dc", "ef")
ROWS_Q = row_table(STEPS_Q)
ROWS_KV = row_table(STEPS_KV)
ROWS_SHARD = shard_table(STEPS_ROWS)


def natural_rows():
    table = np.zeros((DEVICES, 32), np.int32)
    for device in range(DEVICES):
        xs = [p[0] for p in slot_places(device, ("bb", "aa"))]
        table[device] = [x * 8 + shard for shard in range(8) for x in xs]
    return table


ROWS_GU = natural_rows()


def block_table():
    table = np.zeros((DEVICES, 4), np.int32)
    for device in range(DEVICES):
        x, _, _, k = place_of(device)
        own = quarter_of(x, k)
        table[device] = [own, own ^ 1, own ^ 3, own ^ 2]
    return table


BLOCKS = block_table()
X_SLOTS = np.array([[(0, 2, 3, 1)[own ^ x] for x in range(4)] for own in range(4)], np.int32)


def dot(left, right):
    return lax.dot_general(left, right, (((1,), (0,)), ((), ())), preferred_element_type=F32)


def dot_nt(left, right):
    return lax.dot_general(left, right, (((1,), (1,)), ((), ())), preferred_element_type=F32)


def dot_tn(left, right):
    return lax.dot_general(left, right, (((0,), (0,)), ((), ())), preferred_element_type=F32)


def at(index, size):
    return pl.ds(pl.multiple_of(index * size, size), size)


def causal_scores(queries, keys, block):
    scores = dot_nt(queries, keys)
    row = lax.broadcasted_iota(jnp.int32, scores.shape, 0) & (BLOCK - 1)
    col = lax.broadcasted_iota(jnp.int32, scores.shape, 1)
    return jnp.where(col <= row + block * BLOCK, scores, NEG_FILL)


def softmax_rows(scores):
    exponent = jnp.exp(scores - jnp.max(scores, axis=1, keepdims=True))
    return exponent * (1.0 / jnp.sum(exponent, axis=1, keepdims=True))


def attention_kernel(
    rows_q, rows_kv, blocks, n1, w_q, w_kv, cos, sin, gain_q, gain_k, w_all, pre, q_out, k_out, v_out, att
):
    factor = 1.0 / math.sqrt(HD)
    for slot in range(32):
        w_all[at(rows_q[slot], 32), 0:512] = w_q[slot]
        w_all[at(rows_kv[slot], 32), 512:1024] = w_kv[slot]
    for slot in range(4):
        block = blocks[slot]
        here = at(block, BLOCK)
        projected = dot(n1[slot * BLOCK : (slot + 1) * BLOCK, :], w_all[...])
        pre[here, :] = projected[:, :768]
        cos_part = cos[here, :]
        sin_part = sin[here, :]

        def turned(column, gain):
            head = projected[:, column : column + HD]
            normed = head * lax.rsqrt(jnp.mean(head * head, axis=1, keepdims=True) + EPS) * gain[...]
            return normed * cos_part + pltpu.roll(normed, HD // 2, 1) * sin_part

        for head in range(4):
            rotated = (turned(head * HD, gain_q) * factor).astype(BF)
            q_out[head // 2, block, (head % 2) * BLOCK : (head % 2 + 1) * BLOCK, :] = rotated
        for head in range(2):
            k_out[head, here, :] = turned(512 + head * HD, gain_k).astype(BF)
            v_out[head, here, :] = projected[:, 768 + head * HD : 768 + (head + 1) * HD].astype(BF)
    for group in range(2):
        for block in range(4):
            width = (block + 1) * BLOCK
            scores = causal_scores(q_out[group, block], k_out[group, :width, :], block)
            weights = softmax_rows(scores).astype(BF)
            attended = dot(weights, v_out[group, :width, :]).astype(BF)
            own = blocks[0] ^ block
            slot = own ^ (own >> 1)
            for head in range(2):
                column = (group * 2 + head) * HD
                att[at(slot, BLOCK), column : column + HD] = attended[head * BLOCK : (head + 1) * BLOCK]


def attention_back_kernel(
    blocks, grad_state, w_out, queries, keys, values, pre, cos, sin, gain_q, gain_k,
    grad_pre, grad_gain_q, grad_gain_k, grad_att,
):
    factor = 1.0 / math.sqrt(HD)
    for slot in range(4):
        part = dot_nt(grad_state[slot * BLOCK : (slot + 1) * BLOCK, :], w_out[...]).astype(BF)
        for head in range(4):
            grad_att[head // 2, blocks[slot], (head % 2) * BLOCK : (head % 2 + 1) * BLOCK, :] = part[
                :, head * HD : (head + 1) * HD
            ]

    def back_through(grad, head, cos_part, sin_part, gain):
        turned = grad * cos_part - pltpu.roll(grad, HD // 2, 1) * sin_part
        scale = lax.rsqrt(jnp.mean(head * head, axis=1, keepdims=True) + EPS)
        unit = head * scale
        scaled = turned * gain[...]
        grad_head = scale * (scaled - unit * jnp.mean(scaled * unit, axis=1, keepdims=True))
        return grad_head, jnp.sum(turned * unit, axis=0, keepdims=True)

    total_q = jnp.zeros((1, HD), F32)
    total_k = jnp.zeros((1, HD), F32)
    for group in range(2):
        grad_k = [jnp.zeros((BLOCK, HD), F32) for _ in range(4)]
        grad_v = [jnp.zeros((BLOCK, HD), F32) for _ in range(4)]
        for block in range(4):
            width = (block + 1) * BLOCK
            own = blocks[0] ^ block
            there = at(own ^ (own >> 1), BLOCK)
            query = queries[group, block]
            probs = softmax_rows(causal_scores(query, keys[group, :width, :], block))
            grad_o = grad_att[group, block]
            grad_probs = dot_nt(grad_o, values[group, :width, :])
            inner = jnp.sum(probs * grad_probs, axis=1, keepdims=True)
            grad_scores = (probs * (grad_probs - inner)).astype(BF)
            low_probs = probs.astype(BF)
            grad_q = dot(grad_scores, keys[group, :width, :]) * factor
            for head in range(2):
                column = (group * 2 + head) * HD
                grad_head, gain_part = back_through(
                    grad_q[head * BLOCK : (head + 1) * BLOCK],
                    pre[block * BLOCK : (block + 1) * BLOCK, column : column + HD],
                    cos[block * BLOCK : (block + 1) * BLOCK, :],
                    sin[block * BLOCK : (block + 1) * BLOCK, :],
                    gain_q,
                )
                total_q = total_q + gain_part
                grad_pre[there, column : column + HD] = grad_head.astype(BF)
            part_k = dot_tn(grad_scores, query)
            part_v = dot_tn(low_probs, grad_o)
            for key_block in range(block + 1):
                rows = slice(key_block * BLOCK, (key_block + 1) * BLOCK)
                grad_k[key_block] = grad_k[key_block] + part_k[rows]
                grad_v[key_block] = grad_v[key_block] + part_v[rows]
        for block in range(4):
            own = blocks[0] ^ block
            there = at(own ^ (own >> 1), BLOCK)
            column = 512 + group * HD
            grad_head, gain_part = back_through(
                grad_k[block],
                pre[block * BLOCK : (block + 1) * BLOCK, column : column + HD],
                cos[block * BLOCK : (block + 1) * BLOCK, :],
                sin[block * BLOCK : (block + 1) * BLOCK, :],
                gain_k,
            )
            total_k = total_k + gain_part
            grad_pre[there, column : column + HD] = grad_head.astype(BF)
            grad_pre[there, 768 + group * HD : 768 + (group + 1) * HD] = grad_v[block].astype(BF)
    grad_gain_q[...] = total_q
    grad_gain_k[...] = total_k


def out_kernel(rows, att, w_slots, w_out, keep, send):
    for slot in range(8):
        w_out[at(rows[slot], 64), :] = w_slots[slot]
    for slot in range(4):
        part = dot(att[slot * BLOCK : (slot + 1) * BLOCK, :], w_out[...])
        target = keep if slot % 2 == 0 else send
        target[slot // 2] = part.astype(target.dtype)


def mlp_kernel(
    rows_gu, rows_down, n2, grad_mix, w_gu_slots, w_down_slots,
    hidden, grad_gu, mix_keep, mix_send, grad_keep, grad_send, w_gu, w_down,
):
    for slot in range(32):
        w_gu[at(rows_gu[slot], 32), :] = w_gu_slots[slot]
    for slot in range(8):
        w_down[at(rows_down[slot], 96), :] = w_down_slots[slot]
    half = FF // 4
    for slot in range(2):
        here = slice(slot * BLOCK, (slot + 1) * BLOCK)
        gate_up = dot(n2[here, :], w_gu[...])
        grad_hidden = dot_nt(grad_mix[here, :], w_down[...])
        gate = gate_up[:, :half]
        up = gate_up[:, half:]
        sigmoid = 1.0 / (1.0 + jnp.exp(-gate))
        silu = gate * sigmoid
        low_hidden = (silu * up).astype(BF)
        hidden[here, :] = low_hidden
        grad_gate = grad_hidden * up * (sigmoid * (1.0 + gate * (1.0 - sigmoid)))
        low_grad = jnp.concatenate([grad_gate, grad_hidden * silu], axis=1).astype(BF)
        grad_gu[here, :] = low_grad
        mix = mix_keep if slot == 0 else mix_send
        back = grad_keep if slot == 0 else grad_send
        back[...] = dot_nt(low_grad, w_gu[...]).astype(back.dtype)
        mix[...] = dot(low_hidden, w_down[...]).astype(mix.dtype)


def mlp_weights_kernel(
    x_slots, n2_own, n2_far, hidden_own, hidden_far, mix_own, mix_far, gu_own, gu_far, grad_gu, grad_down
):
    for x in range(4):
        here = slice(x * BLOCK, (x + 1) * BLOCK)
        part = dot_tn(n2_own[:, here], gu_own[...]) + dot_tn(n2_far[:, here], gu_far[...])
        grad_gu[:, x_slots[x], :, :] = part.astype(BF).reshape(8, 32, 2 * FF // 4)
    for third in range(3):
        here = slice(third * BLOCK, (third + 1) * BLOCK)
        part = dot_tn(hidden_own[:, here], mix_own[...]) + dot_tn(hidden_far[:, here], mix_far[...])
        grad_down[here, :] = part.astype(BF)


def qkv_weights_kernel(rows_q, rows_kv, n1, grad_pre, grad_q, grad_kv, total):
    for x in range(4):
        here = slice(x * BLOCK, (x + 1) * BLOCK)
        total[here, :] = dot_tn(n1[:, here], grad_pre[...]).astype(BF)
    for slot in range(32):
        grad_q[slot] = total[at(rows_q[slot], 32), 0:512]
        grad_kv[slot] = total[at(rows_kv[slot], 32), 512:1024]


def input_kernel(grad_pre, w_all, keep, send):
    for slot in range(4):
        part = dot_nt(grad_pre[slot * BLOCK : (slot + 1) * BLOCK, :], w_all[...])
        target = keep if slot % 2 == 0 else send
        target[slot // 2] = part.astype(target.dtype)


def call(kernel, outs, args, scalars, scratch=(), flops=0):
    space = [pl.BlockSpec(memory_space=pltpu.SMEM)] * scalars
    space += [pl.BlockSpec(memory_space=pltpu.VMEM)] * (len(args) - scalars)
    size = sum(math.prod(a.shape) * a.dtype.itemsize for a in list(args) + list(outs))
    return pl.pallas_call(
        kernel,
        out_shape=outs,
        in_specs=space,
        out_specs=[pl.BlockSpec(memory_space=pltpu.VMEM)] * len(outs),
        scratch_shapes=list(scratch),
        compiler_params=pltpu.CompilerParams(vmem_limit_bytes=VMEM_LIMIT),
        cost_estimate=pl.CostEstimate(flops=flops, bytes_accessed=size, transcendentals=0),
    )(*args)


def struct(shape, dtype):
    return jax.ShapeDtypeStruct(shape, dtype)


def rms_scale(value, gain):
    return value * lax.rsqrt(jnp.mean(value * value, axis=-1, keepdims=True) + EPS) * gain


def rms_back(value, gain, grad):
    scale = lax.rsqrt(jnp.mean(value * value, axis=-1, keepdims=True) + EPS)
    scaled = grad * gain
    inner = jnp.mean(scaled * value, axis=-1, keepdims=True)
    grad_value = scale * scaled - value * (scale * scale * scale) * inner
    return grad_value, jnp.sum(grad * value * scale, axis=0)


def adamw(weight, gradient, first_moment, second_moment, rate, decay_rate):
    first_moment = BETA_ONE * first_moment + (1.0 - BETA_ONE) * gradient
    second_moment = BETA_TWO * second_moment + (1.0 - BETA_TWO) * gradient * gradient
    first_hat = first_moment / (1.0 - BETA_ONE**STEP)
    second_hat = second_moment / (1.0 - BETA_TWO**STEP)
    weight = weight - rate * (first_hat / (jnp.sqrt(second_hat) + ADAM_EPS) + decay_rate * weight)
    return (weight, first_moment, second_moment)


def fold(value, steps):
    for dims in reversed(steps):
        half = value.shape[0] // 2
        got = swap(value[half:].astype(BF), dims)
        value = value[:half].astype(F32) + got.astype(F32)
    return value


def rounded(value):
    return lax.reduce_precision(value.astype(F32), 8, 7)


def both(value, dims):
    low = rounded(value)
    return low + swap(low.astype(BF), dims).astype(F32)


def pick(stack, index):
    return lax.dynamic_index_in_dim(stack, index, 0, keepdims=False)


def on_device(
    tokens,
    cotangent,
    w_qkv,
    w_out,
    w_gu,
    w_down,
    gains,
    first_qkv,
    first_out,
    first_gu,
    first_down,
    first_gains,
    second_qkv,
    second_out,
    second_gu,
    second_down,
    second_gains,
):
    width = tokens.shape[-1]
    x_at = lax.axis_index("seq")
    shard_at = lax.axis_index("shard")
    replica_at = lax.axis_index("replica")
    device = (x_at * 8 + shard_at) * 4 + replica_at
    core = replica_at % 2
    quarter = jnp.where(x_at < 2, core, 3 - core)
    rows_q = pick(jnp.asarray(ROWS_Q), device)
    rows_kv = pick(jnp.asarray(ROWS_KV), device)
    rows_shard = pick(jnp.asarray(ROWS_SHARD), device)
    rows_gu = pick(jnp.asarray(ROWS_GU), device)
    blocks = pick(jnp.asarray(BLOCKS), device)
    x_slots = pick(jnp.asarray(X_SLOTS), x_at)

    low_qkv = w_qkv.astype(BF)
    stack_q = jnp.stack([low_qkv[:, 512 * n : 512 * (n + 1)] for n in range(4)])
    stack_kv = jnp.stack(
        [
            jnp.concatenate(
                [low_qkv[:, 2048 + 256 * n : 2304 + 256 * n], low_qkv[:, 3072 + 256 * n : 3328 + 256 * n]],
                axis=1,
            )
            for n in range(4)
        ]
    )
    stack_qkv = jnp.concatenate([stack_q, stack_kv], axis=2)
    mine = pick(stack_qkv, quarter)[None]
    mine = jnp.concatenate([mine, swap(pick(stack_qkv, 3 - quarter)[None], "bb")], axis=0)
    mine = jnp.concatenate([mine, swap(mine, "aa")], axis=0)
    slots_q = spread(mine[:, :, :512], STEPS_Q)
    slots_kv = spread(mine[:, :, 512:], STEPS_KV)

    own_tokens = rehome(tokens[0])
    far_tokens = swap(own_tokens, "bb")
    side_tokens = swap(jnp.stack([own_tokens, far_tokens]), "kk")
    all_tokens = jnp.concatenate([own_tokens, side_tokens[0], far_tokens, side_tokens[1]], axis=0)

    spot = (jnp.arange(32) == x_at * 8 + shard_at)[:, None]
    gain_vals = jnp.where(spot, rounded(gains)[None, :], 0.0)
    gain_vals = jnp.pad(gain_vals.reshape(-1), (0, 768)).reshape(24, 128)
    for dims in ("bb", "aa", "cd", "dc", "ef"):
        gain_vals = gain_vals + swap(gain_vals, dims)
    gain_vals = gain_vals.reshape(-1)[: 2 * width + 2 * HD]
    gain_one = gain_vals[:width]
    gain_two = gain_vals[width : 2 * width]
    gain_query = gain_vals[2 * width : 2 * width + HD].reshape(1, HD)
    gain_key = gain_vals[2 * width + HD :].reshape(1, HD)

    slots_out = spread(rehome(w_out.astype(BF))[None], STEPS_ROWS)
    slots_down = spread(rehome(w_down.astype(BF))[None], STEPS_ROWS)

    low_gu = w_gu.astype(BF)
    part = FF // 4
    stack_gu = jnp.stack(
        [
            jnp.concatenate(
                [low_gu[:, part * n : part * (n + 1)], low_gu[:, FF + part * n : FF + part * (n + 1)]], axis=1
            )
            for n in range(4)
        ]
    )
    mine_gu = pick(stack_gu, quarter)[None]
    mine_gu = jnp.concatenate([mine_gu, swap(pick(stack_gu, 3 - quarter)[None], "bb")], axis=0)
    mine_gu = jnp.concatenate([mine_gu, swap(mine_gu, "aa")], axis=0)
    slots_gu = lax.all_gather(mine_gu, "shard", axis=0, tiled=True)

    own_mix = rehome(cotangent[0])
    side_mix = swap(own_mix, "kk")
    near_mix = jnp.concatenate([own_mix, side_mix], axis=0)
    other_mix = swap(own_mix, "bb")
    far_mix = jnp.concatenate([other_mix, swap(other_mix, "kk")], axis=0)

    positions = jnp.arange(4 * BLOCK, dtype=F32)
    frequency = THETA ** (-jnp.arange(HD // 2, dtype=F32) / (HD // 2))
    angles = positions[:, None] * frequency[None, :]
    cos_half, sin_half = jnp.cos(angles), jnp.sin(angles)
    cos_table = jnp.concatenate([cos_half, cos_half], axis=1)
    sin_table = jnp.concatenate([-sin_half, sin_half], axis=1)

    n1 = rms_scale(all_tokens.astype(F32), gain_one).astype(BF)
    total = 4 * BLOCK
    w_all, pre, queries, keys, values, att = call(
        attention_kernel,
        [
            struct((width, 1024), BF),
            struct((total, 768), F32),
            struct((2, 4, 2 * BLOCK, HD), BF),
            struct((2, total, HD), BF),
            struct((2, total, HD), BF),
            struct((total, 512), BF),
        ],
        [rows_q, rows_kv, blocks, n1, slots_q, slots_kv, cos_table, sin_table, gain_query, gain_key],
        3,
        flops=3_600_000_000,
    )
    w_out_all, out_keep, out_send = call(
        out_kernel,
        [struct((512, width), BF), struct((2, BLOCK, width), F32), struct((2, BLOCK, width), BF)],
        [rows_shard, att, slots_out],
        1,
        flops=1_080_000_000,
    )
    out_half = out_keep + swap(out_send, "kk").astype(F32)
    out_full = out_half[0] + swap(out_half[1].astype(BF), "bb").astype(F32)
    inputs = own_tokens.astype(F32)
    state = inputs + out_full
    n2 = rms_scale(state, gain_two).astype(BF)
    near_n2 = jnp.concatenate([n2, swap(n2, "kk")], axis=0)
    other_n2 = swap(n2, "bb")
    far_n2 = jnp.concatenate([other_n2, swap(other_n2, "kk")], axis=0)

    def mlp(n2_part, mix_part):
        return call(
            mlp_kernel,
            [
                struct((2 * BLOCK, part), BF),
                struct((2 * BLOCK, 2 * part), BF),
                struct((BLOCK, width), F32),
                struct((BLOCK, width), BF),
                struct((BLOCK, width), F32),
                struct((BLOCK, width), BF),
            ],
            [rows_gu, rows_shard, n2_part, mix_part, slots_gu, slots_down],
            2,
            scratch=[pltpu.VMEM((width, 2 * part), BF), pltpu.VMEM((part, width), BF)],
            flops=4_840_000_000,
        )

    hidden_own, gu_own, mix_keep_own, mix_send_own, back_keep_own, back_send_own = mlp(near_n2, near_mix)
    hidden_far, gu_far, mix_keep_far, mix_send_far, back_keep_far, back_send_far = mlp(far_n2, far_mix)

    back_far = back_keep_far + swap(back_send_far, "kk").astype(F32)
    back_own = back_keep_own + swap(back_send_own, "kk").astype(F32)
    grad_n2 = back_own + swap(back_far.astype(BF), "bb").astype(F32)
    grad_state_norm, grad_gain_two = rms_back(state, gain_two, grad_n2)
    grad_state = own_mix.astype(F32) + grad_state_norm
    low_state = grad_state.astype(BF)
    far_state = swap(low_state, "bb")
    side_state = swap(jnp.stack([low_state, far_state]), "kk")
    all_state = jnp.concatenate([low_state, side_state[0], far_state, side_state[1]], axis=0)

    grad_gu, grad_down = call(
        mlp_weights_kernel,
        [struct((8, 4, 32, 2 * part), BF), struct((part, width), BF)],
        [x_slots, near_n2, far_n2, hidden_own, hidden_far, near_mix, far_mix, gu_own, gu_far],
        1,
        flops=4_840_000_000,
    )
    grad_down = lax.psum_scatter(grad_down, "shard", scatter_dimension=0, tiled=True)
    grad_gu = lax.psum_scatter(grad_gu, "shard", scatter_dimension=0, tiled=False)

    mix_far_sum = mix_keep_far + swap(mix_send_far, "kk").astype(F32)
    mix_own_sum = mix_keep_own + swap(mix_send_own, "kk").astype(F32)
    mixed = state + mix_own_sum + swap(mix_far_sum.astype(BF), "bb").astype(F32)
    mixed_out = rehome(mixed.astype(BF))[None]

    grad_out = dot_tn(att, all_state).astype(BF)
    grad_out = lax.psum_scatter(grad_out, "shard", scatter_dimension=0, tiled=True)
    grad_pre, grad_gain_query, grad_gain_key = call(
        attention_back_kernel,
        [struct((total, 1024), BF), struct((1, HD), F32), struct((1, HD), F32)],
        [
            blocks, all_state, w_out_all, queries, keys, values, pre, cos_table, sin_table, gain_query, gain_key,
        ],
        1,
        scratch=[pltpu.VMEM((2, 4, 2 * BLOCK, HD), BF)],
        flops=5_000_000_000,
    )
    grad_q_slots, grad_kv_slots = call(
        qkv_weights_kernel,
        [struct((32, 32, 512), BF), struct((32, 32, 512), BF)],
        [rows_q, rows_kv, n1, grad_pre],
        2,
        scratch=[pltpu.VMEM((width, 1024), BF)],
        flops=2_150_000_000,
    )
    in_keep, in_send = call(
        input_kernel,
        [struct((2, BLOCK, width), F32), struct((2, BLOCK, width), BF)],
        [grad_pre, w_all],
        0,
        flops=2_150_000_000,
    )
    in_half = in_keep + swap(in_send, "kk").astype(F32)
    grad_n1 = in_half[0] + swap(in_half[1].astype(BF), "bb").astype(F32)
    grad_input_norm, grad_gain_one = rms_back(inputs, gain_one, grad_n1)
    input_grad = rehome(grad_state + grad_input_norm)[None]

    def of_columns(value):
        value = both(value[:2].astype(F32) + swap(value[2:].astype(BF), "aa").astype(F32), "hh")
        value = rounded(value).astype(BF)
        value = jnp.stack([value[0], swap(value[1], "bb")])
        value = jnp.concatenate([value, swap(value, "kk")], axis=0)
        order = [pick(value, slot) for slot in quarter_slots]
        return [piece.astype(F32) for piece in order]

    quarter_slots = []
    for n in range(4):
        own = quarter ^ n
        quarter_slots.append(jnp.where(own == 0, 0, jnp.where(own == 3, 1, jnp.where(own == 1, 2, 3))))

    def of_rows(value):
        value = rounded(both(both(value, "aa"), "hh")).astype(BF)
        return jnp.where(quarter == x_at, value, swap(value, "kk")).astype(F32)

    own_down = of_rows(grad_down)
    own_out = of_rows(grad_out)
    pieces = of_columns(grad_gu)
    own_gu = jnp.concatenate([p[:, :part] for p in pieces] + [p[:, part:] for p in pieces], axis=1)
    shard_q = fold(grad_q_slots, STEPS_Q)
    shard_kv = fold(grad_kv_slots, STEPS_KV)
    pieces = of_columns(jnp.concatenate([shard_q, shard_kv], axis=2))
    own_qkv = jnp.concatenate(
        [p[:, :512] for p in pieces] + [p[:, 512:768] for p in pieces] + [p[:, 768:] for p in pieces], axis=1
    )
    grad_gains = jnp.concatenate([grad_gain_one, grad_gain_two, grad_gain_query[0], grad_gain_key[0]])
    grad_gains = jnp.pad(grad_gains, (0, 768)).reshape(24, 128)
    for dims in ("ab", "ba", "cd", "dc", "ef", "hh", "kk"):
        grad_gains = grad_gains + swap(grad_gains, dims)
    own_gains = pick(grad_gains.reshape(-1)[: 2 * width + 2 * HD].reshape(32, 72), x_at * 8 + shard_at)

    upd_qkv = adamw(w_qkv, own_qkv, first_qkv, second_qkv, RATES[0], DECAYS[0])
    upd_out = adamw(w_out, own_out, first_out, second_out, RATES[1], DECAYS[1])
    upd_gu = adamw(w_gu, own_gu, first_gu, second_gu, RATES[2], DECAYS[2])
    upd_down = adamw(w_down, own_down, first_down, second_down, RATES[3], DECAYS[3])
    upd_gains = adamw(gains, own_gains, first_gains, second_gains, RATES[4], DECAYS[4])
    return (mixed_out, input_grad, *upd_qkv, *upd_out, *upd_gu, *upd_down, *upd_gains)


def solution(mesh):
    rows = P(("seq", "shard"), None)
    flat = P(("seq", "shard"))
    whole = P(("shard", "replica"), "seq", None)
    per_weight = (rows, rows, rows, rows, flat)
    return jax.shard_map(
        on_device,
        mesh=mesh,
        in_specs=(whole, whole) + per_weight * 3,
        out_specs=(whole, whole) + (rows,) * 12 + (flat,) * 3,
        check_vma=False,
    )
```

time: 1910 us -> 439 us (0.23)
  waiting for transfers between devices: 1300 us -> 122 us
  local copies, waits for them, and re-layouts: 225 us -> 25 us
  blocking collectives: 128 us -> 0 us
  matrix products: 128 us -> 2.25 us
  starting transfers between devices: 0.37 us -> 125 us
  Pallas kernels: 0 us -> 80.2 us
  other arithmetic: 104 us -> 64.5 us
    reduce_scatter x3, waiting for transfers between devices: 705 us -> 0.04 us  [the longest x1 0.02 us: on_device(): lax.psum_scatter(grad_down, 'shard', scatter_dimension=0, tiled=True)]
    all_gather x5 -> x1, waiting for transfers between devices: 485 us -> 0.01 us  [on_device(): slots_gu = lax.all_gather(mine_gu, 'shard', axis=0, tiled=True)]
    dot_general x18 -> x1, matrix products: 128 us -> 2.25 us  [dot_tn(): lax.dot_general(left, right, (((0,), (0,)), ((), ())), preferred_element_...]
    ppermute x0 -> x74, starting transfers between devices: none -> 125 us  [the longest x68 111 us: swap(): return lax.ppermute(value, AXES, partners(dims))]
    ppermute x0 -> x74, waiting for transfers between devices: none -> 121 us  [the longest x68 105 us: swap(): return lax.ppermute(value, AXES, partners(dims))]
    unnamed x10 -> x4, waiting for transfers between devices: 110 us -> 0.71 us
    another operation x6 -> x1, local copies, waits for them, and re-layouts: 84.2 us -> 0.01 us  [on_device(): stack_q = jnp.stack([low_qkv[:, 512 * n:512 * (n + 1)] for n in range(4)])]
    unnamed x2 -> x0, blocking collectives: 81.7 us -> none
  transfers between devices with their start and end apart: 9 -> 78, of which waited for: 8 -> 31; matrix products, arithmetic and copies ran while one was open for 13% -> 20% of each run, Pallas kernels for 0% -> 12%
where the time goes in v1:
time: 439 us; the launch traced here: 434 us
  starting transfers between devices  125 us (28%)
  waiting for transfers between devices  122 us (28%)
  Pallas kernels  80.2 us (18%)
  other arithmetic  64.5 us (15%)
  local copies, waits for them, and re-layouts  25 us (6%)
  between operations  15.3 us (3%)
    ppermute x68, starting transfers between devices, swap(): return lax.ppermute(value, AXES, partners(dims))  111 us
    ppermute x68, waiting for transfers between devices, swap(): return lax.ppermute(value, AXES, partners(dims))  105 us
    pallas_call x8, Pallas kernels, call(): pl.pallas_call(kernel, out_shape=outs, in_specs=space, out_specs=[pl.Bloc...  80.2 us
    ppermute x6, waiting for transfers between devices, rehome(): return lax.ppermute(value, AXES, home_pairs())  16.4 us
    convert_element_type x1, other arithmetic, on_device(): n1 = rms_scale(all_tokens.astype(F32), gain_one).astype(BF)  16.4 us
    ppermute x6, starting transfers between devices, rehome(): return lax.ppermute(value, AXES, home_pairs())  14.4 us
    concatenate x12, other arithmetic, spread(): value = jnp.concatenate([value, swap(value, dims)], axis=0)  12.5 us
  transfers between devices with their start and end apart: 78, of which 31 were waited for; matrix products, arithmetic and copies ran while one was open for 20% of the time, Pallas kernels for 12%

profile of v1, /device:TPU:1, one launch (start us, length us, event | category | flops | bytes accessed | tf_op | source)
XLA Modules:
  0.0 434.4 jit_solution(15999446179624663519)
XLA Ops:
  58.4 6.0 %collective-permute-start.2 = (bf16[2,256,1024]{2,1,0:T(8,128)(2,1)}, bf16[2,256,1024]{2,1,0:T(8,128)(2,1)S(1)}, u32[]{:S(2)}, u32[]{:S(2)}) collective-permute-start(bf16[2,256,1024]{2,1,0:T(8,128)(2,1)} %pad_maximum_fusion.3), channel_id=1, source_target_pairs={{0,1},{1,0},{2,3},{3,2},{4,5},{5,4},{6,7},{7,6},{8,9},{9,8},{10,11... | collective-permute-start | bytes 3145736 | tf_op jit(solution)/shard_map/ppermute | solution.py:68
  80.5 16.4 %fusion.2.n1 = bf16[1024,1024]{1,0:T(8,128)(2,1)} fusion(f32[1024]{0:T(1024)S(1)} %get-tuple-element.145, f32[1024]{0:T(1024)S(1)} %add_rsqrt_fusion, bf16[256,1024]{1,0:T(8,128)(2,1)S(1)} %get-tuple-element.104, bf16[256,1024]{1,0:T(8,128)(2,1)S(1)} %collective-permute-done.1, bf16[256,1024]{1,0:T(8,128)(2,1)S(1)} %get-tuple-element.103, ...), kind=kLoop, calls=%fused_computation.4 | loop fusion | flops 11534336 | bytes 4202496 | tf_op jit(solution)/shard_map/convert_element_type | solution.py:512
  96.9 12.0 %shard_map.350 = (bf16[1024,1024]{1,0:T(8,128)(2,1)}, f32[1024,768]{1,0:T(8,128)}, bf16[2,4,512,128]{3,2,1,0:T(8,128)(2,1)}, bf16[2,1024,128]{2,1,0:T(8,128)(2,1...) custom-call(s32[32]{0:T(128)} %get-tuple-element.155.rows_q, s32[32]{0:T(128)} %get-tuple-element.156.rows_kv, ...), custom_call_target="tpu_custom_call" | custom-call | flops 3600000000 | bytes 13632784 | tf_op jit(solution)/shard_map/pallas_call | solution.py:357
  108.9 4.4 %shard_map.351 = (bf16[512,1024]{1,0:T(8,128)(2,1)}, f32[2,256,1024]{2,1,0:T(8,128)}, bf16[2,256,1024]{2,1,0:T(8,128)(2,1)}) custom-call(s32[8]{0:T(128)} %fusion.35.rows.rows_down, bf16[1024,512]{1,0:T(8,128)(2,1)} %get-tuple-element.47.att, bf16[8,64,1024]{2,1,0:T(8,128)(2,1)} %pad_maximum_fusion.6.w_slots), custom_call_target="tpu_custom_call" | custom-call | flops 1080000000 | bytes 6291488 | tf_op jit(solution)/shard_map/pallas_call | solution.py:357
  119.4 7.3 %collective-permute-done.27 = bf16[96,1024]{1,0:T(8,128)(2,1)S(1)} collective-permute-done((bf16[96,1024]{1,0:T(8,128)(2,1)S(1)}, bf16[96,1024]{1,0:T(8,128)(2,1)S(1)}, u32[]{:S(2)}, u32[]{:S(2)}) %collective-permute-start.27) | collective-permute-done | bytes 196640 | tf_op jit(solution)/shard_map/ppermute | solution.py:81
  145.2 5.5 %collective-permute-done.21 = bf16[256,1024]{1,0:T(8,128)(2,1)S(1)} collective-permute-done((bf16[256,1024]{1,0:T(8,128)(2,1)S(1)}, bf16[256,1024]{1,0:T(8,128)(2,1)S(1)}, u32[]{:S(2)}, u32[]{:S(2)}) %collective-permute-start.21) | collective-permute-done | bytes 524320 | tf_op jit(solution)/shard_map/ppermute | solution.py:68
  158.2 4.1 collective-permute-done.32
  170.8 9.6 %shard_map.353 = (bf16[512,768]{1,0:T(8,128)(2,1)}, bf16[512,1536]{1,0:T(8,128)(2,1)}, f32[256,1024]{1,0:T(8,128)}, bf16[256,1024]{1,0:T(8,128)(2,1)}, f32[256,1024]{1,0:T(8,128)}, /*index=5*/bf16[256,1024]{1,0:T(8,128)(2,1)}) custom-call(s32[32]{0:T(128)} %fusion.39.rows_gu, s32[8]{0:T(128)} %fusion.35.rows.rows_down, ...), custom_call_target="tpu_custom_call" | custom-call | flops 4840000000 | bytes 12320928 | tf_op jit(solution)/shard_map/pallas_call | solution.py:357
  180.4 9.7 %shard_map.352 = (bf16[512,768]{1,0:T(8,128)(2,1)}, bf16[512,1536]{1,0:T(8,128)(2,1)}, f32[256,1024]{1,0:T(8,128)}, bf16[256,1024]{1,0:T(8,128)(2,1)}, f32[256,1024]{1,0:T(8,128)}, /*index=5*/bf16[256,1024]{1,0:T(8,128)(2,1)}) custom-call(s32[32]{0:T(128)} %fusion.39.rows_gu, s32[8]{0:T(128)} %fusion.35.rows.rows_down, ...), custom_call_target="tpu_custom_call" | custom-call | flops 4840000000 | bytes 12320928 | tf_op jit(solution)/shard_map/pallas_call | solution.py:357
  190.1 10.0 %shard_map.357 = (bf16[8,4,32,1536]{3,2,1,0:T(8,128)(2,1)}, bf16[768,1024]{1,0:T(8,128)(2,1)}) custom-call(s32[4]{0:T(128)} %fusion.40.x_slots, bf16[512,1024]{1,0:T(8,128)(2,1)} %pad_maximum_fusion.7.n2.n2_own, bf16[512,1024]{1,0:T(8,128)(2,1)} %constant_dynamic-update-slice_fusion.2.n2.n2_far, bf16[512,768]{1,0:T(8,128)(2,1)} %get-tuple-element.69.hidden_own, ...), custom_call_target="tpu_custom_call" | custom-call | flops 4840000000 | bytes 13631504 | tf_op jit(solution)/shard_map/pallas_call | solution.py:357
  208.4 10.7 %collective-permute-done.41 = bf16[256,1024]{1,0:T(8,128)(2,1)S(1)} collective-permute-done((bf16[256,1024]{1,0:T(8,128)(2,1)S(1)}, bf16[256,1024]{1,0:T(8,128)(2,1)S(1)}, u32[]{:S(2)}, u32[]{:S(2)}) %collective-permute-start.41) | collective-permute-done | bytes 524320 | tf_op jit(solution)/shard_map/ppermute | solution.py:68
  219.7 10.7 %collective-permute-done.37 = bf16[256,1024]{1,0:T(8,128)(2,1)S(1)} collective-permute-done((bf16[256,1024]{1,0:T(8,128)(2,1)S(1)}, bf16[256,1024]{1,0:T(8,128)(2,1)S(1)}, u32[]{:S(2)}, u32[]{:S(2)}) %collective-permute-start.37) | collective-permute-done | bytes 524320 | tf_op jit(solution)/shard_map/ppermute | solution.py:68
  232.7 12.5 %collective-permute-done.42 = bf16[256,1024]{1,0:T(8,128)(2,1)S(1)} collective-permute-done((bf16[256,1024]{1,0:T(8,128)(2,1)S(1)}, bf16[256,1024]{1,0:T(8,128)(2,1)S(1)}, u32[]{:S(2)}, u32[]{:S(2)}) %collective-permute-start.42) | collective-permute-done | bytes 524320 | tf_op jit(solution)/shard_map/ppermute | solution.py:68
  250.4 9.1 %collective-permute-done.38 = bf16[256,1024]{1,0:T(8,128)(2,1)S(1)} collective-permute-done((bf16[256,1024]{1,0:T(8,128)(2,1)}, bf16[256,1024]{1,0:T(8,128)(2,1)S(1)}, u32[]{:S(2)}, u32[]{:S(2)}) %collective-permute-start.38) | collective-permute-done | bytes 524320 | tf_op jit(solution)/shard_map/ppermute | solution.py:81
  263.1 22.7 %shard_map.354 = (bf16[1024,1024]{1,0:T(8,128)(2,1)}, f32[1,128]{1,0:T(1,128)}, f32[1,128]{1,0:T(1,128)}) custom-call(s32[4]{0:T(128)} %fusion.38.blocks, bf16[1024,1024]{1,0:T(8,128)(2,1)} %pad_maximum_fusion.1.grad_state, bf16[512,1024]{1,0:T(8,128)(2,1)} %get-tuple-element.58.w_out, bf16[2,4,512,128]{3,2,1,0:T(8,128)(2,1)} %get-tuple-element.59.queries, ...), custom_call_target="tpu_custom_call" | custom-call | flops 5000000000 | bytes 11536400 | tf_op jit(solution)/shard_map/pallas_call | solution.py:357
  285.7 6.1 %shard_map.356 = (bf16[32,32,512]{2,1,0:T(8,128)(2,1)}, bf16[32,32,512]{2,1,0:T(8,128)(2,1)}) custom-call(s32[32]{0:T(128)} %get-tuple-element.155.rows_q, s32[32]{0:T(128)} %get-tuple-element.156.rows_kv, bf16[1024,1024]{1,0:T(8,128)(2,1)} %fusion.2.n1, bf16[1024,1024]{1,0:T(8,128)(2,1)} %get-tuple-element.63.grad_pre), custom_call_target="tpu_custom_call" | custom-call | flops 2150000128 | bytes 6291712 | tf_op jit(solution)/shard_map/pallas_call | solution.py:357
  298.3 5.8 %shard_map.355 = (f32[2,256,1024]{2,1,0:T(8,128)}, bf16[2,256,1024]{2,1,0:T(8,128)(2,1)}) custom-call(bf16[1024,1024]{1,0:T(8,128)(2,1)} %get-tuple-element.63.grad_pre, bf16[1024,1024]{1,0:T(8,128)(2,1)} %get-tuple-element.64.w_all), custom_call_target="tpu_custom_call" | custom-call | flops 2150000128 | bytes 7340032 | tf_op jit(solution)/shard_map/pallas_call | solution.py:357
  320.8 5.1 %collective-permute-done.49 = bf16[4,32,512]{2,1,0:T(8,128)(2,1)S(1)} collective-permute-done((bf16[4,32,512]{2,1,0:T(8,128)(2,1)S(1)}, bf16[4,32,512]{2,1,0:T(8,128)(2,1)S(1)}, u32[]{:S(2)}, u32[]{:S(2)}) %collective-permute-start.49) | collective-permute-done | bytes 131104 | tf_op jit(solution)/shard_map/ppermute | solution.py:68
  334.2 4.4 %collective-permute-done.54 = bf16[2,32,1024]{2,1,0:T(8,128)(2,1)S(1)} collective-permute-done((bf16[2,32,1024]{2,1,0:T(8,128)(2,1)S(1)}, bf16[2,32,1024]{2,1,0:T(8,128)(2,1)S(1)}, u32[]{:S(2)}, u32[]{:S(2)}) %collective-permute-start.54) | collective-permute-done | bytes 131104 | tf_op jit(solution)/shard_map/ppermute | solution.py:68
  343.1 5.1 %collective-permute-start.56 = (bf16[2,32,1024]{2,1,0:T(8,128)(2,1)S(1)}, bf16[2,32,1024]{2,1,0:T(8,128)(2,1)S(1)}, u32[]{:S(2)}, u32[]{:S(2)}) collective-permute-start(bf16[2,32,1024]{2,1,0:T(8,128)(2,1)S(1)} %pad_maximum_fusion.28), channel_id=1, source_target_pairs={{0,1},{1,0},{2,3},{3,2},{4,5},{5,4},{6,7},{7,6},{8,9},{9,8},{10,11... | collective-permute-start | bytes 393224 | tf_op jit(solution)/shard_map/ppermute | solution.py:68
  373.3 9.9 %collective-permute-start.73 = (f32[24,128]{1,0:T(8,128)S(1)}, f32[24,128]{1,0:T(8,128)S(1)}, u32[]{:S(2)}, u32[]{:S(2)}) collective-permute-start(f32[24,128]{1,0:T(8,128)S(1)} %add.359), channel_id=1, source_target_pairs={{0,1},{1,0},{2,3},{3,2},{4,5},{5,4},{6,7},{7,6},{8,9},{9,8},{10,11... | collective-permute-start | bytes 36872 | tf_op jit(solution)/shard_map/ppermute | solution.py:68
  389.9 13.1 %collective-permute-done.60 = bf16[2,32,1536]{2,1,0:T(8,128)(2,1)S(1)} collective-permute-done((bf16[2,32,1536]{2,1,0:T(8,128)(2,1)S(1)}, bf16[2,32,1536]{2,1,0:T(8,128)(2,1)S(1)}, u32[]{:S(2)}, u32[]{:S(2)}) %collective-permute-start.60) | collective-permute-done | bytes 196640 | tf_op jit(solution)/shard_map/ppermute | solution.py:68
  412.9 4.7 %collective-permute-start.59 = (bf16[64,1024]{1,0:T(8,128)(2,1)S(1)}, bf16[64,1024]{1,0:T(8,128)(2,1)S(1)}, u32[]{:S(2)}, u32[]{:S(2)}) collective-permute-start(bf16[64,1024]{1,0:T(8,128)(2,1)S(1)} %reduce-precision_convert_fusion.2), channel_id=1, source_target_pairs={{0,1},{1,0},{2,3},{3,2},{4,5},{5,4},{6,7},{7,6},{8,9},{9,8},{10,11... | collective-permute-start | bytes 393224 | tf_op jit(solution)/shard_map/ppermute | solution.py:68
  417.6 3.9 collective-permute-start.63
  (376 shorter events, 210.5 us)
Async XLA Ops:
  7.2 163.6 %all-gather.2.cloned.1.call-start = ((), (), s32[]{:S(2)}) async-start(), calls=%async_computation.3 | async-start | bytes 3538944 | tf_op jit(solution)/shard_map/all_gather | solution.py:497
  8.2 15.6 %collective-permute-start.3 = (f32[24,128]{1,0:T(8,128)S(1)}, f32[24,128]{1,0:T(8,128)S(1)}, u32[]{:S(2)}, u32[]{:S(2)}) collective-permute-start(f32[24,128]{1,0:T(8,128)S(1)} %pad_bitcast_fusion), channel_id=1, source_target_pairs={{0,96},{1,97},{2,98},{3,99},{4,100},{5,101},{6,102},{7,103},{8,104... | collective-permute-start | bytes 36872 | tf_op jit(solution)/shard_map/ppermute | solution.py:68
  12.5 29.3 %collective-permute-start.16 = (bf16[64,1024]{1,0:T(8,128)(2,1)S(1)}, bf16[64,1024]{1,0:T(8,128)(2,1)S(1)}, u32[]{:S(2)}, u32[]{:S(2)}) collective-permute-start(bf16[64,1024]{1,0:T(8,128)(2,1)S(1)} %convert_element_type.236), channel_id=1, source_target_pairs={{0,0},{1,32},{2,2},{3,34},{4,4},{5,36},{6,6},{7,38},{8,8},{9,40},{... | collective-permute-start | bytes 393224 | tf_op jit(solution)/shard_map/ppermute | solution.py:81
  16.5 23.2 %collective-permute-start.8 = (bf16[1,32,1024]{2,1,0:T(8,128)(2,1)S(1)}, bf16[1,32,1024]{2,1,0:T(8,128)(2,1)S(1)}, u32[]{:S(2)}, u32[]{:S(2)}) collective-permute-start(bf16[1,32,1024]{2,1,0:T(8,128)(2,1)S(1)} %get-tuple-element.127), channel_id=1, source_target_pairs={{0,96},{1,97},{2,98},{3,99},{4,100},{5,101},{6,102},{7,103},{8,104... | collective-permute-start | bytes 196616 | tf_op jit(solution)/shard_map/ppermute | solution.py:68
  17.6 30.7 %collective-permute-start.25 = (bf16[1,32,1536]{2,1,0:T(8,128)(2,1)S(1)}, bf16[1,32,1536]{2,1,0:T(8,128)(2,1)S(1)}, u32[]{:S(2)}, u32[]{:S(2)}) collective-permute-start(bf16[1,32,1536]{2,1,0:T(8,128)(2,1)S(1)} %get-tuple-element.111), channel_id=1, source_target_pairs={{0,96},{1,97},{2,98},{3,99},{4,100},{5,101},{6,102},{7,103},{8,104... | collective-permute-start | bytes 294920 | tf_op jit(solution)/shard_map/ppermute | solution.py:68
  19.5 28.3 %collective-permute-start = (bf16[256,1024]{1,0:T(8,128)(2,1)S(1)}, bf16[256,1024]{1,0:T(8,128)(2,1)S(1)}, u32[]{:S(2)}, u32[]{:S(2)}) collective-permute-start(bf16[256,1024]{1,0:T(8,128)(2,1)S(1)} %bitcast.165), channel_id=1, source_target_pairs={{0,0},{1,32},{2,2},{3,34},{4,4},{5,36},{6,6},{7,38},{8,8},{9,40},{... | collective-permute-start | bytes 1572872 | tf_op jit(solution)/shard_map/ppermute | solution.py:81
  48.4 22.6 %collective-permute-start.26 = (bf16[2,32,1536]{2,1,0:T(8,128)(2,1)S(1)}, bf16[2,32,1536]{2,1,0:T(8,128)(2,1)S(1)}, u32[]{:S(2)}, u32[]{:S(2)}) collective-permute-start(bf16[2,32,1536]{2,1,0:T(8,128)(2,1)S(1)} %pad_maximum_fusion.25), channel_id=1, source_target_pairs={{0,32},{1,33},{2,34},{3,35},{4,36},{5,37},{6,38},{7,39},{8,40},{9,... | collective-permute-start | bytes 589832 | tf_op jit(solution)/shard_map/ppermute | solution.py:68
  52.3 16.2 %collective-permute-start.11 = (bf16[8,32,512]{2,1,0:T(8,128)(2,1)S(1)}, bf16[8,32,512]{2,1,0:T(8,128)(2,1)S(1)}, u32[]{:S(2)}, u32[]{:S(2)}) collective-permute-start(bf16[8,32,512]{2,1,0:T(8,128)(2,1)S(1)} %pad_maximum_fusion.21), channel_id=1, source_target_pairs={{0,16},{1,19},{2,18},{3,17},{4,20},{5,23},{6,22},{7,21},{8,24},{9,... | collective-permute-start | bytes 786440 | tf_op jit(solution)/shard_map/ppermute | solution.py:68
  55.2 16.6 %collective-permute-start.19 = (bf16[4,64,1024]{2,1,0:T(8,128)(2,1)}, bf16[4,64,1024]{2,1,0:T(8,128)(2,1)}, u32[]{:S(2)}, u32[]{:S(2)}) collective-permute-start(bf16[4,64,1024]{2,1,0:T(8,128)(2,1)} %pad_maximum_fusion.14), channel_id=1, source_target_pairs={{0,16},{1,19},{2,18},{3,17},{4,20},{5,23},{6,22},{7,21},{8,24},{9,... | collective-permute-start | bytes 1572872 | tf_op jit(solution)/shard_map/ppermute | solution.py:68
  58.4 21.6 %collective-permute-start.2 = (bf16[2,256,1024]{2,1,0:T(8,128)(2,1)}, bf16[2,256,1024]{2,1,0:T(8,128)(2,1)S(1)}, u32[]{:S(2)}, u32[]{:S(2)}) collective-permute-start(bf16[2,256,1024]{2,1,0:T(8,128)(2,1)} %pad_maximum_fusion.3), channel_id=1, source_target_pairs={{0,1},{1,0},{2,3},{3,2},{4,5},{5,4},{6,7},{7,6},{8,9},{9,8},{10,11... | collective-permute-start | bytes 3145736 | tf_op jit(solution)/shard_map/ppermute | solution.py:68
  71.8 234.6 %reduce-scatter.8.cloned.1.call-start = ((), (), s32[]{:S(2)}) async-start(), calls=%async_computation.6 | async-start | bytes 1769472 | tf_op jit(solution)/shard_map/reduce_scatter | solution.py:581
  113.3 21.0 %collective-permute-start.20 = (bf16[2,256,1024]{2,1,0:T(8,128)(2,1)}, bf16[2,256,1024]{2,1,0:T(8,128)(2,1)S(1)}, u32[]{:S(2)}, u32[]{:S(2)}) collective-permute-start(bf16[2,256,1024]{2,1,0:T(8,128)(2,1)} %get-tuple-element.49), channel_id=1, source_target_pairs={{0,1},{1,0},{2,3},{3,2},{4,5},{5,4},{6,7},{7,6},{8,9},{9,8},{10,11... | collective-permute-start | bytes 3145736 | tf_op jit(solution)/shard_map/ppermute | solution.py:68
  113.8 19.3 %collective-permute-start.23 = (bf16[256,1024]{1,0:T(8,128)(2,1)S(1)}, bf16[256,1024]{1,0:T(8,128)(2,1)S(1)}, u32[]{:S(2)}, u32[]{:S(2)}) collective-permute-start(bf16[256,1024]{1,0:T(8,128)(2,1)S(1)} %bitcast.166), channel_id=1, source_target_pairs={{0,0},{1,32},{2,2},{3,34},{4,4},{5,36},{6,6},{7,38},{8,8},{9,40},{... | collective-permute-start | bytes 1572872 | tf_op jit(solution)/shard_map/ppermute | solution.py:81
  138.0 19.1 %collective-permute-start.24 = (bf16[256,1024]{1,0:T(8,128)(2,1)S(1)}, bf16[256,1024]{1,0:T(8,128)(2,1)}, u32[]{:S(2)}, u32[]{:S(2)}) collective-permute-start(bf16[256,1024]{1,0:T(8,128)(2,1)S(1)} %collective-permute-done.23), channel_id=1, source_target_pairs={{0,1},{1,0},{2,3},{3,2},{4,5},{5,4},{6,7},{7,6},{8,9},{9,8},{10,11... | collective-permute-start | bytes 1572872 | tf_op jit(solution)/shard_map/ppermute | solution.py:68
  141.0 23.6 %collective-permute-start.30 = (bf16[4,96,1024]{2,1,0:T(8,128)(2,1)}, bf16[4,96,1024]{2,1,0:T(8,128)(2,1)}, u32[]{:S(2)}, u32[]{:S(2)}) collective-permute-start(bf16[4,96,1024]{2,1,0:T(8,128)(2,1)} %pad_maximum_fusion.9), channel_id=1, source_target_pairs={{0,16},{1,19},{2,18},{3,17},{4,20},{5,23},{6,22},{7,21},{8,24},{9,... | collective-permute-start | bytes 2359304 | tf_op jit(solution)/shard_map/ppermute | solution.py:68
  145.2 17.5 %collective-permute-start.35 = (bf16[256,1024]{1,0:T(8,128)(2,1)}, bf16[256,1024]{1,0:T(8,128)(2,1)}, u32[]{:S(2)}, u32[]{:S(2)}) collective-permute-start(bf16[256,1024]{1,0:T(8,128)(2,1)} %collective-permute-done.34), channel_id=1, source_target_pairs={{0,1},{1,0},{2,3},{3,2},{4,5},{5,4},{6,7},{7,6},{8,9},{9,8},{10,11... | collective-permute-start | bytes 1572872 | tf_op jit(solution)/shard_map/ppermute | solution.py:68
  200.1 186.2 %reduce-scatter.6.cloned.1.call-start = ((), (), s32[]{:S(2)}) async-start(), calls=%async_computation.5 | async-start | bytes 3538944 | tf_op jit(solution)/shard_map/reduce_scatter | solution.py:582
  200.9 186.5 %reduce-scatter.4.cloned.1.call-start = ((), (), s32[]{:S(2)}) async-start(), calls=%async_computation.4 | async-start | bytes 1179648 | tf_op jit(solution)/shard_map/reduce_scatter | solution.py:590
  206.5 23.9 %collective-permute-start.37 = (bf16[256,1024]{1,0:T(8,128)(2,1)S(1)}, bf16[256,1024]{1,0:T(8,128)(2,1)S(1)}, u32[]{:S(2)}, u32[]{:S(2)}) collective-permute-start(bf16[256,1024]{1,0:T(8,128)(2,1)S(1)} %add_convert_fusion.2), channel_id=1, source_target_pairs={{0,96},{1,97},{2,98},{3,99},{4,100},{5,101},{6,102},{7,103},{8,104... | collective-permute-start | bytes 1572872 | tf_op jit(solution)/shard_map/ppermute | solution.py:68
  304.1 28.4 %collective-permute-start.44 = (bf16[2,256,1024]{2,1,0:T(8,128)(2,1)}, bf16[2,256,1024]{2,1,0:T(8,128)(2,1)}, u32[]{:S(2)}, u32[]{:S(2)}) collective-permute-start(bf16[2,256,1024]{2,1,0:T(8,128)(2,1)} %get-tuple-element.66), channel_id=1, source_target_pairs={{0,1},{1,0},{2,3},{3,2},{4,5},{5,4},{6,7},{7,6},{8,9},{9,8},{10,11... | collective-permute-start | bytes 3145736 | tf_op jit(solution)/shard_map/ppermute | solution.py:68
  328.4 19.8 %collective-permute-start.66 = (bf16[96,1024]{1,0:T(8,128)(2,1)S(1)}, bf16[96,1024]{1,0:T(8,128)(2,1)S(1)}, u32[]{:S(2)}, u32[]{:S(2)}) collective-permute-start(bf16[96,1024]{1,0:T(8,128)(2,1)S(1)} %reduce-precision_convert_fusion), channel_id=1, source_target_pairs={{0,1},{1,0},{2,3},{3,2},{4,5},{5,4},{6,7},{7,6},{8,9},{9,8},{10,11... | collective-permute-start | bytes 589832 | tf_op jit(solution)/shard_map/ppermute | solution.py:68
  383.6 38.9 %collective-permute-start.46 = (f32[256,1024]{1,0:T(8,128)S(1)}, f32[256,1024]{1,0:T(8,128)S(1)}, u32[]{:S(2)}, u32[]{:S(2)}) collective-permute-start(f32[256,1024]{1,0:T(8,128)S(1)} %fusion.6), channel_id=1, source_target_pairs={{0,0},{1,32},{2,2},{3,34},{4,4},{5,36},{6,6},{7,38},{8,8},{9,40},{... | collective-permute-start | bytes 3145736 | tf_op jit(solution)/shard_map/ppermute | solution.py:81
  387.3 15.7 %collective-permute-start.60 = (bf16[2,32,1536]{2,1,0:T(8,128)(2,1)S(1)}, bf16[2,32,1536]{2,1,0:T(8,128)(2,1)S(1)}, u32[]{:S(2)}, u32[]{:S(2)}) collective-permute-start(bf16[2,32,1536]{2,1,0:T(8,128)(2,1)S(1)} %slice_bitcast_fusion.6), channel_id=1, source_target_pairs={{0,32},{1,33},{2,34},{3,35},{4,36},{5,37},{6,38},{7,39},{8,40},{9,... | collective-permute-start | bytes 589832 | tf_op jit(solution)/shard_map/ppermute | solution.py:68
  388.4 16.1 %collective-permute-start.57 = (bf16[64,1024]{1,0:T(8,128)(2,1)S(1)}, bf16[64,1024]{1,0:T(8,128)(2,1)S(1)}, u32[]{:S(2)}, u32[]{:S(2)}) collective-permute-start(bf16[64,1024]{1,0:T(8,128)(2,1)S(1)} %fusion.30), channel_id=1, source_target_pairs={{0,32},{1,33},{2,34},{3,35},{4,36},{5,37},{6,38},{7,39},{8,40},{9,... | collective-permute-start | bytes 393224 | tf_op jit(solution)/shard_map/ppermute | solution.py:68
  (94 other events, 881.1 us)
Sparse Core Ops, SparseCore 0:
  71.9 38.9 all-gather.1
  200.3 33.2 reduce-scatter.7
  236.0 46.1 reduce-scatter.5
  306.5 31.8 reduce-scatter.3
